TPU v7x, 32 devices: a whole 2x2x4 slice. The times are simulated.
32 devices in a mesh: row: 4 (over z), col: 8 (over y, x, core).
Axes of the slice: x: 2, y: 2, z: 4, core: 2. Of those that a mesh axis runs over, the one named last changes fastest.
Arguments:
- velocity_modes: bfloat16 [3, 2, 2, 2048, 1024], P(None, None, None, 'col', 'row'), may hold values from -6 to 6
- offsets: int32 [1024], P('row'), may hold values from 0 to 2047
- shear_steps: int32 [1], replicated, may hold values from 0 to 31
Outputs:
- advanced: bfloat16 [3, 2, 2, 2048, 1024], P(None, None, None, 'col', 'row')
All inputs are finite; a program needn't handle non-finite values.
Results may differ from a plain program's by a relative error of at most 0.0085.
Values may be sent and summed in bfloat16 or wider, within the bound.
A program may use at most 128 MiB of HBM per device.

v0:
```python
import math

import jax
import jax.numpy as jnp
from jax import lax
from jax.sharding import PartitionSpec as P

dt_step = 0.1
period = 32.0
pair_table = ((0, 1, 2), (1, 3, 4), (2, 4, 5))
first_ids = (0, 0, 0, 1, 1, 2)
second_ids = (0, 1, 2, 1, 2, 2)


def shifted(block, axis, distance):
    devices = range(lax.axis_size(axis))
    route = [((i - distance) % len(devices), i) for i in devices]
    return lax.ppermute(block, axis, route)


def split_table(matrix):
    upper_part = matrix.astype(jnp.bfloat16)
    lower_part = (matrix - upper_part.astype(jnp.float32)).astype(jnp.bfloat16)
    return (upper_part, lower_part)


def apply_split(form, parts, values):
    return jnp.einsum(form, parts[0], values, preferred_element_type=jnp.float32) + jnp.einsum(
        form, parts[1], values, preferred_element_type=jnp.float32
    )


def y_apply(items, length, sign):
    point_ids = jnp.arange(length, dtype=jnp.int32)
    angles = (
        2.0
        * math.pi
        / length
        * (point_ids[:, None] * point_ids[None, :] % length).astype(jnp.float32)
    )
    cosine = split_table(jnp.cos(angles) / math.sqrt(length))
    sine_part = split_table(sign * jnp.sin(angles) / math.sqrt(length))
    real_in = items[:, 0]
    imag_in = items[:, 1]
    form = "vy,czym->czvm"
    real_out = apply_split(form, cosine, real_in) - apply_split(form, sine_part, imag_in)
    imag_out = apply_split(form, sine_part, real_in) + apply_split(form, cosine, imag_in)
    return jnp.stack([real_out, imag_out], 1).astype(jnp.bfloat16)


def x_inverse(items, x_count):
    kx_total = items.shape[-1]
    wave_ids = jnp.arange(kx_total, dtype=jnp.int32)
    points = jnp.arange(x_count, dtype=jnp.int32)
    weights = jnp.where(wave_ids == 0, 1.0, 2.0).astype(jnp.float32) / math.sqrt(x_count)
    angles = (
        2.0
        * math.pi
        / x_count
        * (points[:, None] * wave_ids[None, :] % x_count).astype(jnp.float32)
    )
    cosine = split_table(weights * jnp.cos(angles))
    sine_part = split_table(-weights * jnp.sin(angles))
    form = "xk,czyk->czyx"
    return apply_split(form, cosine, items[:, 0]) + apply_split(form, sine_part, items[:, 1])


def x_forward(products, x_count):
    kx_total = x_count // 2
    wave_ids = jnp.arange(kx_total, dtype=jnp.int32)
    points = jnp.arange(x_count, dtype=jnp.int32)
    angles = (
        2.0
        * math.pi
        / x_count
        * (wave_ids[:, None] * points[None, :] % x_count).astype(jnp.float32)
    )
    cosine = split_table(jnp.cos(angles) / math.sqrt(x_count))
    sine_part = split_table(-jnp.sin(angles) / math.sqrt(x_count))
    form = "kx,ezyx->ezyk"
    real_out = apply_split(form, cosine, products)
    imag_out = apply_split(form, sine_part, products)
    return jnp.stack([real_out, imag_out], 1).astype(jnp.bfloat16)


def shift_lines(spectrum, offsets, y_local, y_count):
    current = spectrum
    bit_count = y_count.bit_length() - 1
    for bit_index in range(bit_count):
        stride = 1 << bit_index
        chosen = offsets // stride % 2 == 1
        if stride < y_local:
            edge_rows = shifted(current[:, :, :, :stride, :], "col", -1)
            rolled = jnp.concatenate([current[:, :, :, stride:, :], edge_rows], axis=3)
        else:
            rolled = shifted(current, "col", -(stride // y_local))
        current = jnp.where(chosen[None, None, None, None, :], rolled, current)
    return current


def advance(state_modes, modes, kx_ids, ky_ids, strain, x_count, y_count):
    ky_signed = (ky_ids + y_count // 2) % y_count - y_count // 2
    two_pi = 2.0 * math.pi
    kx_wave = two_pi * kx_ids.astype(jnp.float32) / x_count
    ky_wave = two_pi * ky_signed.astype(jnp.float32) / y_count - strain * kx_wave
    retain = ((3 * kx_ids < x_count) & (3 * jnp.abs(ky_signed) < y_count)).astype(jnp.float32)
    update = []
    for l in range(3):
        flux_real = kx_wave * modes[pair_table[l][0], 0].astype(jnp.float32) + ky_wave * modes[
            pair_table[l][1], 0
        ].astype(jnp.float32)
        flux_imag = kx_wave * modes[pair_table[l][0], 1].astype(jnp.float32) + ky_wave * modes[
            pair_table[l][1], 1
        ].astype(jnp.float32)
        update.append(jnp.stack([flux_imag, -flux_real]))
    update = jnp.stack(update)
    return (state_modes.astype(jnp.float32) + dt_step * retain * update).astype(jnp.bfloat16)


def local(velocity_modes, offsets, shear_steps):
    y_local = velocity_modes.shape[3]
    kx_local = velocity_modes.shape[4]
    row_count = lax.axis_size("row")
    col_count = lax.axis_size("col")
    y_count = y_local * col_count
    kx_total = kx_local * row_count
    x_count = 2 * kx_total
    strain = shear_steps[0].astype(jnp.float32) / period - 0.5
    remeshed = shift_lines(velocity_modes, offsets, y_local, y_count)
    y_lines = y_apply(
        lax.all_to_all(remeshed, "col", split_axis=4, concat_axis=3, tiled=True), y_count, 1.0
    )
    velocity = x_inverse(
        lax.all_to_all(y_lines, ("row", "col"), split_axis=3, concat_axis=4, tiled=True), x_count
    )
    products = jnp.stack(
        [velocity[first_ids[e]] * velocity[second_ids[e]] for e in range(6)]
    ).astype(jnp.bfloat16)
    x_modes = x_forward(products, x_count)
    y_modes = y_apply(
        lax.all_to_all(x_modes, ("row", "col"), split_axis=4, concat_axis=3, tiled=True),
        y_count,
        -1.0,
    )
    back_modes = lax.all_to_all(y_modes, "col", split_axis=3, concat_axis=4, tiled=True)
    kx_ids = (lax.axis_index("row") * kx_local + jnp.arange(kx_local, dtype=jnp.int32))[
        None, None, :
    ]
    ky_ids = (lax.axis_index("col") * y_local + jnp.arange(y_local, dtype=jnp.int32))[None, :, None]
    return advance(remeshed, back_modes, kx_ids, ky_ids, strain, x_count, y_count)


def solution(mesh):
    return jax.shard_map(
        local,
        mesh=mesh,
        in_specs=(P(None, None, None, "col", "row"), P("row"), P()),
        out_specs=P(None, None, None, "col", "row"),
        check_vma=False,
    )
```

profile of v0, /device:TPU:11, one launch (start us, length us, event | category | flops | bytes accessed | tf_op | source)
XLA Modules:
  0.0 1828.7 jit_solution(16001642794144493387)
XLA Ops:
  101.5 34.8 %collective-permute-done.9 = bf16[3,2,2,256,256]{3,4,2,1,0:T(8,128)(2,1)S(1)} collective-permute-done((bf16[3,2,2,256,256]{3,4,2,1,0:T(8,128)(2,1)S(1)}, bf16[3,2,2,256,256]{3,4,2,1,0:T(8,128)(2,1)S(1)}, u32[]{:S(2)}, u32[]{:S(2)}) %collective-permute-start.9) | collective-permute-done | bytes 1572896 | tf_op jit(solution)/shard_map/ppermute | solution.py:18
  137.8 34.9 %collective-permute-done.10 = bf16[3,2,2,256,256]{3,4,2,1,0:T(8,128)(2,1)S(1)} collective-permute-done((bf16[3,2,2,256,256]{3,4,2,1,0:T(8,128)(2,1)S(1)}, bf16[3,2,2,256,256]{3,4,2,1,0:T(8,128)(2,1)S(1)}, u32[]{:S(2)}, u32[]{:S(2)}) %collective-permute-start.10) | collective-permute-done | bytes 1572896 | tf_op jit(solution)/shard_map/ppermute | solution.py:18
  174.6 24.0 %all_to_all.72 = bf16[3,2,2,256,256]{3,2,1,0,4:T(2,128)(2,1)S(1)} all-to-all(bf16[3,2,2,256,256]{3,2,1,0,4:T(2,128)(2,1)S(1)} %copy.63), channel_id=1, replica_groups=mesh['row'=4,'col'=8] {'col'}, dimensions={4} | all-to-all | bytes 3145728 | tf_op jit(solution)/shard_map/all_to_all | solution.py:131
  202.9 64.1 %fusion.30 = f32[3,2,32,2048]{3,2,1,0:T(8,128)S(1)} fusion(bf16[3,2,2048,32]{2,3,1,0:T(8,128)(2,1)S(1)} %slice_bitcast_fusion.87), kind=kOutput, calls=%fused_computation.50 | convolution fusion | flops 1690304512 | bytes 2359296 | tf_op jit(solution)/shard_map/vy,czym->czvm/dot_general | solution.py:28
  267.0 64.8 %fusion.46 = f32[3,2,32,2048]{3,2,1,0:T(8,128)S(1)} fusion(bf16[3,2,2048,32]{2,3,1,0:T(8,128)(2,1)S(1)} %slice_bitcast_fusion.93), kind=kOutput, calls=%fused_computation.58 | convolution fusion | flops 1690304512 | bytes 2359296 | tf_op jit(solution)/shard_map/vy,czym->czvm/dot_general | solution.py:28
  331.9 64.4 %fusion.28 = f32[3,2,32,2048]{3,2,1,0:T(8,128)S(1)} fusion(bf16[3,2,2048,32]{2,3,1,0:T(8,128)(2,1)S(1)} %slice_bitcast_fusion.86), kind=kOutput, calls=%fused_computation.49 | convolution fusion | flops 1690304512 | bytes 2359296 | tf_op jit(solution)/shard_map/vy,czym->czvm/dot_general | solution.py:28
  396.2 64.9 %fusion.44 = f32[3,2,32,2048]{3,2,1,0:T(8,128)S(1)} fusion(bf16[3,2,2048,32]{2,3,1,0:T(8,128)(2,1)S(1)} %slice_bitcast_fusion.92), kind=kOutput, calls=%fused_computation.57 | convolution fusion | flops 1690304512 | bytes 2359296 | tf_op jit(solution)/shard_map/vy,czym->czvm/dot_general | solution.py:28
  461.2 64.2 %fusion.128 = f32[3,2,32,2048]{3,2,1,0:T(8,128)S(1)} fusion(f32[3,2,32,2048]{3,2,1,0:T(8,128)S(1)} %fusion.30, bf16[3,2,2048,32]{2,3,1,0:T(8,128)(2,1)S(1)} %slice_bitcast_fusion.96), kind=kOutput, calls=%fused_computation.109 | convolution fusion | flops 1678114816 | bytes 3932160 | tf_op jit(solution)/shard_map/vy,czym->czvm/dot_general | solution.py:28
  525.4 63.9 %fusion.131 = f32[3,2,32,2048]{3,2,1,0:T(8,128)S(1)} fusion(f32[3,2,32,2048]{3,2,1,0:T(8,128)S(1)} %fusion.28, bf16[3,2,2048,32]{2,3,1,0:T(8,128)(2,1)S(1)} %slice_bitcast_fusion.97), kind=kOutput, calls=%fused_computation.110 | convolution fusion | flops 1678114816 | bytes 3932160 | tf_op jit(solution)/shard_map/vy,czym->czvm/dot_general | solution.py:28
  589.3 64.3 %fusion.140 = bf16[3,1,2,2048,32]{3,4,2,0,1:T(8,128)(2,1)S(1)} fusion(f32[3,2,32,2048]{3,2,1,0:T(8,128)S(1)} %fusion.128, f32[3,2,32,2048]{3,2,1,0:T(8,128)S(1)} %fusion.46, bf16[3,2,2048,32]{2,3,1,0:T(8,128)(2,1)S(1)} %copy-done.3), kind=kOutput, calls=%fused_computation.113 | convolution fusion | flops 1678901248 | bytes 4718592 | tf_op jit(solution)/shard_map/vy,czym->czvm/dot_general | solution.py:28
  653.7 64.6 %fusion.143 = bf16[3,1,2,2048,32]{3,4,2,0,1:T(8,128)(2,1)S(1)} fusion(f32[3,2,32,2048]{3,2,1,0:T(8,128)S(1)} %fusion.131, f32[3,2,32,2048]{3,2,1,0:T(8,128)S(1)} %fusion.44, bf16[3,2,2048,32]{2,3,1,0:T(8,128)(2,1)S(1)} %copy-done.4), kind=kOutput, calls=%fused_computation.114 | convolution fusion | flops 1678901248 | bytes 4718592 | tf_op jit(solution)/shard_map/vy,czym->czvm/dot_general | solution.py:28
  748.8 36.3 %all-to-all-done.1 = bf16[32,2,12288]{2,1,0:T(2,128)(2,1)S(1)} async-done(((bf16[32,2,12288]{2,1,0:T(2,128)(2,1)}), bf16[32,2,12288]{2,1,0:T(2,128)(2,1)S(1)}, u32[]{:S(2)}, u32[]{:S(2)}) %all-to-all-start.1) | async-done | bytes 1572896 | tf_op jit(solution)/shard_map/all_to_all | solution.py:134
  803.1 31.7 %fusion.68 = f32[3,2,64,2048]{3,2,1,0:T(8,128)S(1)} fusion(f32[1024]{0:T(1024)S(1)} %select_multiply_fusion, bf16[3,2,2,64,1024]{3,4,2,1,0:T(8,128)(2,1)S(1)} %bitcast.413), kind=kOutput, calls=%fused_computation.74 | convolution fusion | flops 1644167168 | bytes 4722688 | tf_op jit(solution)/shard_map/xk,czyk->czyx/dot_general | solution.py:28
  834.8 32.4 %fusion.75 = f32[3,2,64,2048]{3,2,1,0:T(8,128)S(1)} fusion(f32[1024]{0:T(1024)S(1)} %select_multiply_fusion, bf16[3,2,2,64,1024]{3,4,2,1,0:T(8,128)(2,1)S(1)} %bitcast.414), kind=kOutput, calls=%fused_computation.78 | convolution fusion | flops 1650458624 | bytes 4722688 | tf_op jit(solution)/shard_map/xk,czyk->czyx/dot_general | solution.py:28
  867.2 31.8 %fusion.70 = f32[3,2,64,2048]{3,2,1,0:T(8,128)S(1)} fusion(f32[1024]{0:T(1024)S(1)} %fusion.171, bf16[3,2,2,64,1024]{3,4,2,1,0:T(8,128)(2,1)S(1)} %bitcast.415), kind=kOutput, calls=%fused_computation.75 | convolution fusion | flops 1644167168 | bytes 4722688 | tf_op jit(solution)/shard_map/xk,czyk->czyx/dot_general | solution.py:28
  899.0 32.8 %add_add_fusion = f32[3,2,64,2048]{3,2,1,0:T(8,128)S(1)} fusion(f32[3,2,64,2048]{3,2,1,0:T(8,128)S(1)} %fusion.70, f32[3,2,64,2048]{3,2,1,0:T(8,128)S(1)} %fusion.68, f32[3,2,64,2048]{3,2,1,0:T(8,128)S(1)} %fusion.75, f32[1024]{0:T(1024)S(1)} %fusion.171, bf16[3,2,2,64,1024]{3,4,2,1,0:T(8,128)(2,1)S(1)} %bitcast.416), kind=kOutput, calls=%fused_computation.102 | convolution fusion | flops 1652817920 | bytes 14159872 | tf_op jit(solution)/shard_map/xk,czyk->czyx/dot_general | solution.py:28
  932.4 32.8 %fusion.72 = f32[6,2,64,1024]{3,2,1,0:T(8,128)S(1)} fusion(bf16[6,2,64,2048]{3,2,1,0:T(8,128)(2,1)S(1)} %fusion.167), kind=kOutput, calls=%fused_computation.76 | convolution fusion | flops 3254779904 | bytes 6291456 | tf_op jit(solution)/shard_map/kx,ezyx->ezyk/dot_general | solution.py:28
  965.2 33.2 %fusion.66 = f32[6,2,64,1024]{3,2,1,0:T(8,128)S(1)} fusion(bf16[6,2,64,2048]{3,2,1,0:T(8,128)(2,1)S(1)} %fusion.167), kind=kOutput, calls=%fused_computation.73 | convolution fusion | flops 3256877056 | bytes 6291456 | tf_op jit(solution)/shard_map/kx,ezyx->ezyk/dot_general | solution.py:28
  998.4 33.5 %fusion.150 = bf16[6,1,2,64,1024]{4,3,2,0,1:T(8,128)(2,1)S(1)} fusion(f32[6,2,64,1024]{3,2,1,0:T(8,128)S(1)} %fusion.72, bf16[6,2,64,2048]{3,2,1,0:T(8,128)(2,1)S(1)} %fusion.167), kind=kOutput, calls=%fused_computation.131 | convolution fusion | flops 3262644224 | bytes 7864320 | tf_op jit(solution)/shard_map/kx,ezyx->ezyk/dot_general | solution.py:28
  1031.9 33.7 %fusion.153 = bf16[6,1,2,64,1024]{4,3,2,0,1:T(8,128)(2,1)S(1)} fusion(f32[6,2,64,1024]{3,2,1,0:T(8,128)S(1)} %fusion.66, bf16[6,2,64,2048]{3,2,1,0:T(8,128)(2,1)S(1)} %fusion.167), kind=kOutput, calls=%fused_computation.132 | convolution fusion | flops 3264741376 | bytes 7864320 | tf_op jit(solution)/shard_map/kx,ezyx->ezyk/dot_general | solution.py:28
  1085.0 75.5 %all_to_all.73 = bf16[32,2,24576]{2,1,0:T(2,128)(2,1)} all-to-all(bf16[32,2,24576]{2,1,0:T(2,128)(2,1)S(1)} %reshape.373), channel_id=1, replica_groups=mesh['row'=4,'col'=8] {'row','col'}, dimensions={0} | all-to-all | bytes 6291456 | tf_op jit(solution)/shard_map/all_to_all | solution.py:141
  1189.9 65.1 %fusion.26 = f32[6,2,32,2048]{3,2,1,0:T(8,128)S(1)} fusion(bf16[6,2,2048,32]{2,3,1,0:T(8,128)(2,1)S(1)} %slice_bitcast_fusion.85), kind=kOutput, calls=%fused_computation.48 | convolution fusion | flops 3300917248 | bytes 4718592 | tf_op jit(solution)/shard_map/vy,czym->czvm/dot_general | solution.py:28
  1254.9 64.5 %fusion.34 = f32[6,2,32,2048]{3,2,1,0:T(8,128)S(1)} fusion(bf16[6,2,2048,32]{2,3,1,0:T(8,128)(2,1)S(1)} %slice_bitcast_fusion.89), kind=kOutput, calls=%fused_computation.52 | convolution fusion | flops 3288334336 | bytes 4718592 | tf_op jit(solution)/shard_map/vy,czym->czvm/dot_general | solution.py:28
  1319.5 65.8 %fusion.42 = f32[6,2,32,2048]{3,2,1,0:T(8,128)S(1)} fusion(bf16[6,2,2048,32]{2,3,1,0:T(8,128)(2,1)S(1)} %slice_bitcast_fusion.91), kind=kOutput, calls=%fused_computation.56 | convolution fusion | flops 3300917248 | bytes 4718592 | tf_op jit(solution)/shard_map/vy,czym->czvm/dot_general | solution.py:28
  1385.2 65.7 %fusion.24 = f32[6,2,32,2048]{3,2,1,0:T(8,128)} fusion(bf16[6,2,2048,32]{2,3,1,0:T(8,128)(2,1)S(1)} %slice_bitcast_fusion.84), kind=kOutput, calls=%fused_computation.47 | convolution fusion | flops 3300917248 | bytes 4718592 | tf_op jit(solution)/shard_map/vy,czym->czvm/dot_general | solution.py:28
  1451.0 64.4 %fusion.32 = f32[6,2,32,2048]{3,2,1,0:T(8,128)S(1)} fusion(bf16[6,2,2048,32]{2,3,1,0:T(8,128)(2,1)S(1)} %slice_bitcast_fusion.88), kind=kOutput, calls=%fused_computation.51 | convolution fusion | flops 3288334336 | bytes 4718592 | tf_op jit(solution)/shard_map/vy,czym->czvm/dot_general | solution.py:28
  1515.4 65.6 %fusion.40 = f32[6,2,32,2048]{3,2,1,0:T(8,128)S(1)} fusion(bf16[6,2,2048,32]{2,3,1,0:T(8,128)(2,1)S(1)} %slice_bitcast_fusion.90), kind=kOutput, calls=%fused_computation.55 | convolution fusion | flops 3300917248 | bytes 4718592 | tf_op jit(solution)/shard_map/vy,czym->czvm/dot_general | solution.py:28
  1581.0 65.3 %fusion.110 = bf16[6,1,2,2048,32]{3,4,2,0,1:T(8,128)(2,1)S(1)} fusion(f32[6,2,32,2048]{3,2,1,0:T(8,128)S(1)} %fusion.42, f32[6,2,32,2048]{3,2,1,0:T(8,128)S(1)} %fusion.34, f32[6,2,32,2048]{3,2,1,0:T(8,128)S(1)} %fusion.26, bf16[6,2,2048,32]{2,3,1,0:T(8,128)(2,1)S(1)} %slice_bitcast_fusion.94), kind=kOutput, calls=%fused_computation.103 | convolution fusion | flops 3291480064 | bytes 12582912 | tf_op jit(solution)/shard_map/vy,czym->czvm/dot_general | solution.py:28
  1646.4 65.1 %fusion.113 = bf16[6,1,2,2048,32]{3,4,2,0,1:T(8,128)(2,1)S(1)} fusion(f32[6,2,32,2048]{3,2,1,0:T(8,128)S(1)} %fusion.32, f32[6,2,32,2048]{3,2,1,0:T(8,128)S(1)} %copy-done.5, f32[6,2,32,2048]{3,2,1,0:T(8,128)S(1)} %fusion.40, bf16[6,2,2048,32]{2,3,1,0:T(8,128)(2,1)S(1)} %copy-done.2), kind=kOutput, calls=%fused_computation.104 | convolution fusion | flops 3291480064 | bytes 12582912 | tf_op jit(solution)/shard_map/vy,czym->czvm/dot_general | solution.py:28
  1711.8 22.4 %copy.73 = bf16[6,2,2,2048,32]{4,2,0,1,3:T(2,128)(2,1)} copy(bf16[6,2,2,2048,32]{3,4,2,0,1:T(8,128)(2,1)S(1)} %pad_maximum_fusion.1) | data formatting | bytes 6291456 | tf_op jit(solution)/shard_map/stack | solution.py:48
  1754.6 34.6 %all-to-all-done.3 = bf16[8,2,98304]{2,1,0:T(2,128)(2,1)S(1)} async-done(((bf16[8,2,98304]{2,1,0:T(2,128)(2,1)}), bf16[8,2,98304]{2,1,0:T(2,128)(2,1)S(1)}, u32[]{:S(2)}, u32[]{:S(2)}) %all-to-all-start.3) | async-done | bytes 3145760 | tf_op jit(solution)/shard_map/all_to_all | solution.py:145
  1797.8 26.6 %copy.92 = bf16[6,2,2,8,256,32]{4,5,3,2,1,0:T(8,128)(2,1)S(1)} copy(bf16[6,2,2,8,256,32]{5,2,0,1,4,3:T(2,128)(2,1)} %bitcast.405) | data formatting | bytes 6291456 | tf_op jit(solution)/shard_map/all_to_all | solution.py:145
  (131 shorter events, 239.3 us)
Async XLA Ops:
  0.8 6.2 collective-permute-start
  11.1 4.0 collective-permute-start.1
  19.2 4.2 collective-permute-start.2
  27.4 4.4 collective-permute-start.3
  35.8 5.0 collective-permute-start.4
  44.7 6.3 collective-permute-start.5
  54.9 8.3 collective-permute-start.6
  67.5 12.4 collective-permute-start.7
  80.4 20.8 %collective-permute-start.8 = (bf16[3,2,2,256,256]{3,4,2,1,0:T(8,128)(2,1)S(1)}, bf16[3,2,2,256,256]{3,4,2,1,0:T(8,128)(2,1)S(1)}, u32[]{:S(2)}, u32[]{:S(2)}) collective-permute-start(bf16[3,2,2,256,256]{3,4,2,1,0:T(8,128)(2,1)S(1)} %maximum_select_fusion.7), channel_id=1, source_target_pairs={{1,0},{2,1},{3,2},{4,3},{5,4},{6,5},{7,6},{0,7},{9,8},{10,9},{11,1... | collective-permute-start | bytes 4718600 | tf_op jit(solution)/shard_map/ppermute | solution.py:18
  101.4 34.8 %collective-permute-start.9 = (bf16[3,2,2,256,256]{3,4,2,1,0:T(8,128)(2,1)S(1)}, bf16[3,2,2,256,256]{3,4,2,1,0:T(8,128)(2,1)S(1)}, u32[]{:S(2)}, u32[]{:S(2)}) collective-permute-start(bf16[3,2,2,256,256]{3,4,2,1,0:T(8,128)(2,1)S(1)} %broadcast_select_fusion), channel_id=1, source_target_pairs={{2,0},{3,1},{4,2},{5,3},{6,4},{7,5},{0,6},{1,7},{10,8},{11,9},{12,... | collective-permute-start | bytes 4718600 | tf_op jit(solution)/shard_map/ppermute | solution.py:18
  136.5 36.2 %collective-permute-start.10 = (bf16[3,2,2,256,256]{3,4,2,1,0:T(8,128)(2,1)S(1)}, bf16[3,2,2,256,256]{3,4,2,1,0:T(8,128)(2,1)S(1)}, u32[]{:S(2)}, u32[]{:S(2)}) collective-permute-start(bf16[3,2,2,256,256]{3,4,2,1,0:T(8,128)(2,1)S(1)} %broadcast_select_fusion.1), channel_id=1, source_target_pairs={{4,0},{5,1},{6,2},{7,3},{0,4},{1,5},{2,6},{3,7},{12,8},{13,9},{14,... | collective-permute-start | bytes 4718600 | tf_op jit(solution)/shard_map/ppermute | solution.py:18
  173.0 25.9 %copy-start = (bf16[3,2,2,256,256]{3,4,2,1,0:T(8,128)(2,1)}, bf16[3,2,2,256,256]{3,4,2,1,0:T(8,128)(2,1)S(1)}, u32[]{:S(2)}) copy-start(bf16[3,2,2,256,256]{3,4,2,1,0:T(8,128)(2,1)S(1)} %broadcast_select_fusion.2) | copy-start | bytes 4718596
  525.4 63.9 %copy-start.3 = (bf16[3,2,2048,32]{2,3,1,0:T(8,128)(2,1)S(1)}, bf16[3,2,2048,32]{2,3,1,0:T(8,128)(2,1)}, u32[]{:S(2)}) copy-start(bf16[3,2,2048,32]{2,3,1,0:T(8,128)(2,1)} %slice_bitcast_fusion.98) | copy-start | bytes 2359300
  589.3 64.4 %copy-start.4 = (bf16[3,2,2048,32]{2,3,1,0:T(8,128)(2,1)S(1)}, bf16[3,2,2048,32]{2,3,1,0:T(8,128)(2,1)}, u32[]{:S(2)}) copy-start(bf16[3,2,2048,32]{2,3,1,0:T(8,128)(2,1)} %slice_bitcast_fusion.99) | copy-start | bytes 2359300
  743.4 41.7 %all-to-all-start.1 = ((bf16[32,2,12288]{2,1,0:T(2,128)(2,1)}), bf16[32,2,12288]{2,1,0:T(2,128)(2,1)S(1)}, u32[]{:S(2)}, u32[]{:S(2)}) async-start(bf16[32,2,12288]{2,1,0:T(2,128)(2,1)} %reshape.371), calls=%async_computation.1 | async-start | bytes 3145728 | tf_op jit(solution)/shard_map/all_to_all | solution.py:134
  1581.0 65.4 %copy-start.2 = (bf16[6,2,2048,32]{2,3,1,0:T(8,128)(2,1)S(1)}, bf16[6,2,2048,32]{2,3,1,0:T(8,128)(2,1)}, u32[]{:S(2)}) copy-start(bf16[6,2,2048,32]{2,3,1,0:T(8,128)(2,1)} %slice_bitcast_fusion.95) | copy-start | bytes 4718596
  1581.0 65.4 %copy-start.5 = (f32[6,2,32,2048]{3,2,1,0:T(8,128)S(1)}, f32[6,2,32,2048]{3,2,1,0:T(8,128)}, u32[]{:S(2)}) copy-start(f32[6,2,32,2048]{3,2,1,0:T(8,128)} %fusion.24) | copy-start | bytes 9437188
  1748.6 40.6 %all-to-all-start.3 = ((bf16[8,2,98304]{2,1,0:T(2,128)(2,1)}), bf16[8,2,98304]{2,1,0:T(2,128)(2,1)S(1)}, u32[]{:S(2)}, u32[]{:S(2)}) async-start(bf16[8,2,98304]{2,1,0:T(2,128)(2,1)} %reshape.375), calls=%async_computation.3 | async-start | bytes 6291456 | tf_op jit(solution)/shard_map/all_to_all | solution.py:145
  1824.5 2.0 copy-start.1
where the time goes:
time: 1840 us; the launch traced here: 1830 us
  matrix products  1300 us (71%)
  local copies, waits for them, and re-layouts  197 us (11%)
  waiting for transfers between devices  195 us (11%)
  blocking collectives  99.5 us (5%)
  other arithmetic  23.9 us (1%)
    dot_general x12, matrix products, apply_split(): jnp.einsum(form, parts[1], values, preferred_element_type=jnp.float32)  653 us
    dot_general x12, matrix products, apply_split(): jnp.einsum(form, parts[0], values, preferred_element_type=jnp.float32)  646 us
    ppermute x11, waiting for transfers between devices, shifted(): return lax.ppermute(block, axis, route)  124 us
    all_to_all x1, blocking collectives, local(): lax.all_to_all(x_modes, ('row', 'col'), split_axis=4, concat_axis=3, tile...  75.5 us
    unnamed x20, local copies, waits for them, and re-layouts  59.6 us
  transfers between devices with their start and end apart: 13, of which 12 were waited for; matrix products, arithmetic and copies ran while one was open for 1% of the time, Pallas kernels for 0%

commit v1 on v0

v1 whole, which is shorter than its diff:
```python
import functools
import math

import jax
import jax.numpy as jnp
import ml_dtypes
import numpy as np
from jax import lax
from jax.experimental import pallas as pl
from jax.experimental.pallas import tpu as pltpu
from jax.sharding import PartitionSpec as P

dt_step = 0.1
period = 32.0
pair_table = ((0, 1), (1, 3), (2, 4))
pairs = ((0, 0), (0, 1), (0, 2), (1, 1), (1, 2))
n_pairs = len(pairs)
bf16 = jnp.bfloat16
f32 = jnp.float32


def waves(rows, columns, length):
    angles = (2.0 * math.pi / length) * ((rows[:, None] * columns[None, :]) % length)
    scale = 1.0 / math.sqrt(length)
    return np.cos(angles) * scale, np.sin(angles) * scale


def narrow(matrix):
    return matrix.astype(ml_dtypes.bfloat16)


def y_table(length, columns):
    cosine, sine = waves(np.arange(length), columns, length)
    return narrow(np.concatenate([cosine, sine], 1))


def x_inverse_table(length, kb):
    ids = np.arange(length // 2)
    cosine, sine = waves(np.arange(length), ids, length)
    weight = np.where(ids == 0, 1.0, 2.0)
    both = np.stack([cosine * weight, -sine * weight], 1)
    both = both.reshape(length, 2, length // 2 // kb, kb).transpose(0, 2, 1, 3)
    return narrow(both.reshape(length, length))


def x_forward_table(length, kb, kept):
    cosine, sine = waves(np.arange(kept * kb), np.arange(length), length)
    both = np.stack([cosine, -sine]).reshape(2, kept, kb, length).transpose(1, 0, 2, 3)
    return narrow(both.reshape(kept * 2 * kb, length))


def exchange_kernel(rows, cols, wide, kept, cid, in_ref, out_ref, send_sem, recv_sem, own_sem):
    row, col = lax.axis_index("row"), lax.axis_index("col")
    count = rows * cols if wide else cols
    me = row * cols + col if wide else col

    def place(d):
        return (d // cols, d % cols) if wide else (row, d)

    barrier = pltpu.get_barrier_semaphore()

    def greet(s, c):
        other = (me + s) % count
        pl.semaphore_signal(
            barrier, inc=1, device_id=place(other), device_id_type=pl.DeviceIdType.MESH
        )
        return c

    lax.fori_loop(1, count, greet, 0)
    pl.semaphore_wait(barrier, count - 1)

    def copy(s):
        other = (me + s) % count
        source = (me + count - s) % count
        send = pltpu.make_async_remote_copy(
            src_ref=in_ref.at[jnp.minimum(other, kept - 1)],
            dst_ref=out_ref.at[me],
            send_sem=send_sem.at[s],
            recv_sem=recv_sem.at[s],
            device_id=place(other),
            device_id_type=pl.DeviceIdType.MESH,
        )
        return other, source, send

    own = pltpu.make_async_copy(in_ref.at[jnp.minimum(me, kept - 1)], out_ref.at[me], own_sem)

    def begin(s, c):
        other, _, send = copy(s)

        @pl.when(other < kept)
        def _():
            send.start()

        return c

    lax.fori_loop(1, count, begin, 0)
    own.start()
    own.wait()

    def finish(s, c):
        other, _, send = copy(s)

        @pl.when(other < kept)
        def _():
            send.wait_send()

        @pl.when(me < kept)
        def _():
            send.wait_recv()

        return c

    lax.fori_loop(1, count, finish, 0)


def exchange(blocks, rows, cols, wide, cid):
    count = rows * cols if wide else cols
    kept = blocks.shape[0]
    return pl.pallas_call(
        functools.partial(exchange_kernel, rows, cols, wide, kept, cid),
        out_shape=jax.ShapeDtypeStruct((count,) + blocks.shape[1:], blocks.dtype),
        in_specs=[pl.BlockSpec(memory_space=pl.ANY)],
        out_specs=pl.BlockSpec(memory_space=pl.ANY),
        scratch_shapes=[
            pltpu.SemaphoreType.DMA((count,)),
            pltpu.SemaphoreType.DMA((count,)),
            pltpu.SemaphoreType.DMA,
        ],
        compiler_params=pltpu.CompilerParams(collective_id=cid, has_side_effects=True),
    )(blocks)


def roll_kernel(length, offs_ref, in_ref, out_ref):
    value = jnp.concatenate(
        [in_ref[s, 0].astype(f32) for s in range(in_ref.shape[0])], axis=1
    )
    offs = offs_ref[...]
    stride = 1
    while stride < length:
        chosen = (offs // stride) % 2 == 1
        value = jnp.where(chosen, pltpu.roll(value, length - stride, 1), value)
        stride *= 2
    out_ref[0] = value.astype(out_ref.dtype)


def remesh(blocks, offs):
    sources, groups, kb, yl = blocks.shape
    length = sources * yl
    return pl.pallas_call(
        functools.partial(roll_kernel, length),
        grid=(groups,),
        out_shape=jax.ShapeDtypeStruct((groups, kb, length), blocks.dtype),
        in_specs=[
            pl.BlockSpec((kb, 1), lambda i: (0, 0)),
            pl.BlockSpec((sources, 1, kb, yl), lambda i: (0, i, 0, 0)),
        ],
        out_specs=pl.BlockSpec((1, kb, length), lambda i: (i, 0, 0)),
    )(offs.reshape(kb, 1), blocks)


def dot(a, b):
    return jnp.dot(a, b, preferred_element_type=f32)


def local(velocity_modes, offsets, shear_steps):
    nz, yl, kl = velocity_modes.shape[2:]
    rows, cols = lax.axis_size("row"), lax.axis_size("col")
    devices = rows * cols
    ny, nk = yl * cols, kl * rows
    nx = 2 * nk
    kb = kl // cols
    gb = ny * nz // devices
    gn = ny // gb
    row, col = lax.axis_index("row"), lax.axis_index("col")
    strain = shear_steps[0].astype(f32) / period - 0.5

    parts = velocity_modes.reshape(6 * nz, yl, cols, kb).transpose(2, 0, 3, 1)
    parts = exchange(parts, rows, cols, False, 1)
    offs = lax.dynamic_slice(offsets, (col * kb,), (kb,))
    remeshed = remesh(parts, offs)

    every = np.arange(ny)
    both = dot(remeshed.reshape(-1, ny), jnp.asarray(y_table(ny, every)))
    both = both.reshape(3, 2, nz, kb, 2, ny)
    real = both[:, 0, :, :, 0] - both[:, 1, :, :, 1]
    imag = both[:, 0, :, :, 1] + both[:, 1, :, :, 0]
    lines = jnp.stack([real, imag]).astype(bf16).reshape(2, 3, nz, kb, gn, gb)
    lines = lines.transpose(2, 4, 0, 3, 1, 5).reshape(devices, 2 * kb, 3 * gb)
    lines = exchange(lines, rows, cols, True, 2).reshape(2 * nk, 3 * gb)

    velocity = dot(jnp.asarray(x_inverse_table(nx, kb)), lines)
    v = [velocity[:, c * gb : (c + 1) * gb] for c in range(3)]
    products = jnp.concatenate([(v[a] * v[b]).astype(bf16) for a, b in pairs], 1)
    kept = -(-(-(-nx // 3)) // kb)
    x_modes = dot(jnp.asarray(x_forward_table(nx, kb, kept)), products).astype(bf16)
    x_modes = x_modes.reshape(kept, 2 * kb, n_pairs * gb)
    x_modes = exchange(x_modes, rows, cols, True, 3)

    x_modes = x_modes.reshape(nz, gn, 2, kb, n_pairs, gb).transpose(4, 2, 0, 3, 1, 5)
    low = -(-(-(-ny // 3)) // 128) * 128
    near = np.concatenate([np.arange(low), np.arange(ny - low, ny)])
    both = dot(x_modes.reshape(-1, ny), jnp.asarray(y_table(ny, near)))
    both = both.reshape(n_pairs, 2, nz, kb, 2, 2 * low)
    real = both[:, 0, :, :, 0] + both[:, 1, :, :, 1]
    imag = both[:, 1, :, :, 0] - both[:, 0, :, :, 1]

    kx = ((row * cols + col) * kb + jnp.arange(kb, dtype=jnp.int32))[:, None]
    ys = jnp.concatenate(
        [jnp.arange(low, dtype=jnp.int32), jnp.arange(-low, 0, dtype=jnp.int32)]
    )[None, :]
    k1 = 2.0 * math.pi * kx.astype(f32) / nx
    k2 = 2.0 * math.pi * ys.astype(f32) / ny - strain * k1
    retain = (3 * kx < nx) & (3 * jnp.abs(ys) < ny)
    update = []
    for l in range(3):
        e0, e1 = pair_table[l]
        flux_real = k1 * real[e0] + k2 * real[e1]
        flux_imag = k1 * imag[e0] + k2 * imag[e1]
        update.append(jnp.stack([flux_imag, -flux_real]))
    update = jnp.where(retain, dt_step * jnp.stack(update), 0.0)
    state = remeshed.reshape(3, 2, nz, kb, ny)
    advanced = jnp.concatenate(
        [
            (state[..., :low].astype(f32) + update[..., :low]).astype(bf16),
            state[..., low : ny - low],
            (state[..., ny - low :].astype(f32) + update[..., low:]).astype(bf16),
        ],
        -1,
    )
    parts = advanced.reshape(6 * nz, kb, cols, yl).transpose(2, 0, 1, 3)
    parts = exchange(parts, rows, cols, False, 4)
    out = parts.transpose(1, 3, 0, 2)
    return out.reshape(3, 2, nz, yl, kl)


def solution(mesh):
    return jax.shard_map(
        local,
        mesh=mesh,
        in_specs=(P(None, None, None, "col", "row"), P("row"), P()),
        out_specs=P(None, None, None, "col", "row"),
        check_vma=False,
    )
```

time: 1840 us -> 242 us (0.13)
  matrix products: 1300 us -> 36.3 us
  waiting for transfers between devices: 195 us -> 0 us
  local copies, waits for them, and re-layouts: 197 us -> 31.4 us
  Pallas kernels: 0 us -> 163 us
  blocking collectives: 99.5 us -> 0 us
    dot_general x24 -> x4, matrix products: 1300 us -> 36.3 us  [dot(): return jnp.dot(a, b, preferred_element_type=f32)]
    pallas_call x0 -> x5, Pallas kernels: none -> 163 us  [the longest x4 152 us: exchange(): pl.pallas_call(functools.partial(exchange_kernel, rows, cols, wide, kept,...]
    ppermute x11 -> x0, waiting for transfers between devices: 124 us -> none  [shifted(): return lax.ppermute(block, axis, route)]
    all_to_all x2 -> x0, blocking collectives: 99.5 us -> none  [the longest x1 75.5 us: local(): lax.all_to_all(x_modes, ('row', 'col'), split_axis=4, concat_axis=3, tile...]
    all_to_all x2 -> x0, waiting for transfers between devices: 70.9 us -> none  [the longest x1 36.3 us: local(): lax.all_to_all(y_lines, ('row', 'col'), split_axis=3, concat_axis=4, tile...]
    all_to_all x8 -> x0, local copies, waits for them, and re-layouts: 60.1 us -> none  [the longest x1 26.6 us: local(): lax.all_to_all(y_modes, 'col', split_axis=3, concat_axis=4, tiled=True)]
    unnamed x20 -> x10, local copies, waits for them, and re-layouts: 59.6 us -> 4.29 us
    another operation x3 -> x0, local copies, waits for them, and re-layouts: 45 us -> none  [the longest x2 33.5 us: y_apply(): return jnp.stack([real_out, imag_out], 1).astype(jnp.bfloat16)]
  transfers between devices with their start and end apart: 13 -> 0, of which waited for: 12 -> 0; matrix products, arithmetic and copies ran while one was open for 1% -> 0% of each run, Pallas kernels for 0% -> 0%
where the time goes in v1:
time: 242 us; the launch traced here: 241 us
  Pallas kernels  163 us (67%)
  matrix products  36.3 us (15%)
  local copies, waits for them, and re-layouts  31.4 us (13%)
  other arithmetic  8.96 us (4%)
    pallas_call x4, Pallas kernels, exchange(): pl.pallas_call(functools.partial(exchange_kernel, rows, cols, wide, kept,...  152 us
    dot_general x4, matrix products, dot(): return jnp.dot(a, b, preferred_element_type=f32)  36.3 us
    pallas_call x1, Pallas kernels, remesh(): pl.pallas_call(functools.partial(roll_kernel, length), grid=(groups,), ou...  10.9 us
    reshape x1, local copies, waits for them, and re-layouts, local(): x_modes.reshape(nz, gn, 2, kb, n_pairs, gb).transpose(4, 2, 0, 3, 1, 5)  6.99 us

profile of v1, /device:TPU:11, one launch (start us, length us, event | category | flops | bytes accessed | tf_op | source)
XLA Modules:
  0.0 241.0 jit_solution(5194268501910032649)
XLA Ops:
  0.0 0.7 copy-done
  0.8 0.7 copy.36.offs_ref
  1.4 1.7 copy.34
  3.2 1.3 copy.62
  4.5 21.3 %shard_map.73.in_ref = bf16[8,12,32,256]{3,2,1,0:T(8,128)(2,1)} custom-call(bf16[8,12,32,256]{3,2,1,0:T(8,128)(2,1)} %bitcast.147), custom_call_target="tpu_custom_call" | custom-call | tf_op jit(solution)/shard_map/pallas_call | solution.py:119
  25.8 10.9 %shard_map.74 = bf16[12,32,2048]{2,1,0:T(8,128)(2,1)} custom-call(s32[32,1]{1,0:T(8,128)} %copy.36.offs_ref, bf16[8,12,32,256]{3,2,1,0:T(8,128)(2,1)} %shard_map.73.in_ref), custom_call_target="tpu_custom_call" | custom-call | tf_op jit(solution)/shard_map/pallas_call | solution.py:149
  36.7 10.7 %fusion.31 = f32[3,2,2,32,2,2048]{5,3,4,2,1,0:T(8,128)S(1)} fusion(bf16[3,2,2,32,2048,1]{4,3,5,2,1,0:T(8,128)(2,1)} %bitcast.153, bf16[2,2048,2048,1,1,1]{2,1,0,5,4,3:T(8,128)(2,1)} %constant.63), kind=kOutput, calls=%fused_computation.73 | convolution fusion | flops 6442450944 | bytes 24641536 | tf_op jit(solution)/shard_map/dot_general | solution.py:162
  47.4 0.4 fusion.6
  48.0 0.7 copy.37
  48.9 0.7 copy.38
  49.6 1.4 maximum_bitcast_fusion
  50.9 2.5 %reshape.183.in_ref = bf16[32,64,384]{2,1,0:T(8,128)(2,1)} reshape(bf16[2,16,2,32,3,128]{5,4,3,2,1,0:T(4,128)(2,1)S(1)} %maximum_bitcast_fusion) | data formatting | bytes 3145728 | tf_op jit(solution)/shard_map/reshape | solution.py:188
  53.5 38.2 %shard_map.75 = bf16[32,64,384]{2,1,0:T(8,128)(2,1)} custom-call(bf16[32,64,384]{2,1,0:T(8,128)(2,1)} %reshape.183.in_ref), custom_call_target="tpu_custom_call" | custom-call | tf_op jit(solution)/shard_map/pallas_call | solution.py:119
  91.7 6.6 %fusion.32 = f32[2048,384]{0,1:T(8,128)S(1)} fusion(bf16[2048,2048]{1,0:T(8,128)(2,1)} %constant.56.clone, bf16[2048,384]{1,0:T(8,128)(2,1)} %bitcast.160), kind=kOutput, calls=%fused_computation.74 | convolution fusion | flops 3221225472 | bytes 13107200 | tf_op jit(solution)/shard_map/dot_general | solution.py:162
  98.8 7.0 %fusion = bf16[1408,640]{0,1:T(8,128)(2,1)S(1)} fusion(bf16[2048,640]{0,1:T(8,128)(2,1)S(1)} %fusion.13, bf16[1408,2048]{1,0:T(8,128)(2,1)} %constant.57.clone), kind=kOutput, calls=%fused_computation.1 | convolution fusion | flops 3691888640 | bytes 10190848 | tf_op jit(solution)/shard_map/dot_general | solution.py:162
  105.8 2.3 copy.39
  108.1 66.6 %shard_map.76 = bf16[32,64,640]{2,1,0:T(8,128)(2,1)} custom-call(bf16[22,64,640]{2,1,0:T(8,128)(2,1)} %bitcast.145), custom_call_target="tpu_custom_call" | custom-call | tf_op jit(solution)/shard_map/pallas_call | solution.py:119
  174.7 7.0 %reshape.186 = bf16[2,16,2,32,5,128]{5,4,3,2,1,0:T(8,128)(2,1)} reshape(bf16[32,64,640]{2,1,0:T(8,128)(2,1)} %shard_map.76) | data formatting | bytes 5242880 | tf_op jit(solution)/shard_map/reshape | solution.py:199
  181.7 4.1 %copy.40 = bf16[5,2,2,32,16,128]{5,4,3,2,1,0:T(8,128)(2,1)S(1)} copy(bf16[5,2,2,32,16,128]{5,0,3,1,4,2:T(8,128)(2,1)} %bitcast.144) | data formatting | bytes 5242880 | tf_op jit(solution)/shard_map/transpose | solution.py:199
  185.8 3.1 %reshape.191 = bf16[5,2,2,32,2048,1]{4,3,2,1,0,5:T(8,128)(2,1)} reshape(bf16[5,2,2,32,16,128]{5,4,3,2,1,0:T(8,128)(2,1)S(1)} %copy.40) | data formatting | bytes 5242880 | tf_op jit(solution)/shard_map/dot_general | solution.py:162
  188.9 12.0 %fusion.1 = f32[5,2,2,32,2,1536]{5,3,4,2,1,0:T(8,128)S(1)} fusion(bf16[2,1536,2048,1,1,1]{2,1,0,5,4,3:T(8,128)(2,1)} %constant.64, bf16[5,2,2,32,2048,1]{4,3,2,1,0,5:T(8,128)(2,1)} %reshape.191), kind=kOutput, calls=%fused_computation.2 | convolution fusion | flops 8053063680 | bytes 23068672 | tf_op jit(solution)/shard_map/dot_general | solution.py:162
  201.2 1.5 fusion.40
  202.7 1.6 slice_add_fusion
  205.1 2.0 fusion.30
  207.5 0.3 fusion.3
  207.8 1.1 copy-done.2
  208.9 0.3 fusion.8
  209.5 0.5 copy.58
  210.0 1.5 copy.61
  211.5 26.4 %shard_map.77 = bf16[8,12,32,256]{3,2,1,0:T(8,128)(2,1)} custom-call(bf16[8,12,32,256]{3,2,1,0:T(8,128)(2,1)} %bitcast.149), custom_call_target="tpu_custom_call" | custom-call | tf_op jit(solution)/shard_map/pallas_call | solution.py:119
  237.9 1.6 copy.48
  239.5 1.6 copy.49
  (26 shorter events, 1.8 us)
Async XLA Ops:
  0.0 0.7 copy-start
  207.5 1.4 copy-start.2
  237.9 3.2 %copy-start.1 = (s32[256]{0:T(256)S(1)}, s32[256]{0:T(256)}, u32[]{:S(2)}) copy-start(s32[256]{0:T(256)} %param.8) | copy-start | bytes 3076

commit v2 on v1

--- a/solution.py
+++ b/solution.py
@@ -162,6 +162,320 @@
     return jnp.dot(a, b, preferred_element_type=f32)
 
 
+def greet_all(count, me, place):
+    barrier = pltpu.get_barrier_semaphore()
+
+    def greet(s, c):
+        pl.semaphore_signal(
+            barrier,
+            inc=1,
+            device_id=place((me + s) % count),
+            device_id_type=pl.DeviceIdType.MESH,
+        )
+        return c
+
+    lax.fori_loop(1, count, greet, 0)
+    return lambda: pl.semaphore_wait(barrier, count - 1)
+
+
+def back_kernel(
+    rows, cols, nx, ny, nz,
+    modes_ref, state_ref, strain_ref, table_ref, out_ref,
+    table, lines, block, table_sem, send_sem, recv_sem, own_sem,
+):
+    row, col = lax.axis_index("row"), lax.axis_index("col")
+    groups, kb, _ = state_ref.shape
+    yl = ny // cols
+    half = table_ref.shape[0] // 2
+    gn = modes_ref.shape[0] // nz
+    gb = modes_ref.shape[2] // n_pairs
+    first_k = (row * cols + col) * kb
+    wait_all = greet_all(cols, col, lambda d: (row, d))
+    live = 3 * first_k < nx
+
+    def fetch(i):
+        return pltpu.make_async_copy(table_ref.at[i], table.at[i], table_sem.at[i])
+
+    for i in range(2 * half):
+        fetch(i).start()
+    for e in range(n_pairs):
+        for p in range(2):
+            for z in range(nz):
+                top = ((e * 2 + p) * nz + z) * kb
+                for b in range(gn):
+                    lines[top : top + kb, b * gb : (b + 1) * gb] = modes_ref[
+                        z * gn + b, p * kb : (p + 1) * kb, e * gb : (e + 1) * gb
+                    ]
+    for i in range(2 * half):
+        fetch(i).wait()
+    wait_all()
+
+    def send(s):
+        other = (col + s) % cols
+        return pltpu.make_async_remote_copy(
+            src_ref=block.at[other],
+            dst_ref=out_ref.at[col],
+            send_sem=send_sem.at[s],
+            recv_sem=recv_sem.at[s],
+            device_id=(row, other),
+            device_id_type=pl.DeviceIdType.MESH,
+        )
+
+    def make(j):
+        kept = live & ((j < half) | (j >= cols - half))
+        columns = pl.ds(pl.multiple_of(j * yl, yl), yl)
+
+        @pl.when(kept)
+        def _():
+            i = jnp.where(j < half, j, j - (cols - 2 * half))
+            both = dot(lines[...], table[i])
+            kx = first_k + lax.broadcasted_iota(jnp.int32, (kb, yl), 0)
+            ky = j * yl + lax.broadcasted_iota(jnp.int32, (kb, yl), 1)
+            ys = jnp.where(ky < ny // 2, ky, ky - ny)
+            k1 = (2.0 * math.pi / nx) * kx.astype(f32)
+            k2 = (2.0 * math.pi / ny) * ys.astype(f32) - strain_ref[...] * k1
+            retain = (3 * kx < nx) & (3 * jnp.abs(ys) < ny)
+
+            def mode(e, z):
+                a = both[((e * 2) * nz + z) * kb : ((e * 2) * nz + z + 1) * kb]
+                b = both[((e * 2 + 1) * nz + z) * kb : ((e * 2 + 1) * nz + z + 1) * kb]
+                return a[:, :yl] + b[:, yl:], b[:, :yl] - a[:, yl:]
+
+            for z in range(nz):
+                found = [mode(e, z) for e in range(n_pairs)]
+                for l in range(3):
+                    e0, e1 = pair_table[l]
+                    flux_real = k1 * found[e0][0] + k2 * found[e1][0]
+                    flux_imag = k1 * found[e0][1] + k2 * found[e1][1]
+                    for p, update in ((0, flux_imag), (1, -flux_real)):
+                        g = (l * 2 + p) * nz + z
+                        state = state_ref[g, :, columns].astype(f32)
+                        change = jnp.where(retain, dt_step * update, 0.0)
+                        block[j, g] = (state + change).astype(bf16)
+
+        @pl.when(jnp.logical_not(kept))
+        def _():
+            for g in range(groups):
+                block[j, g] = state_ref[g, :, columns]
+
+    def step(s, c):
+        make((col + s) % cols)
+        send(s).start()
+        return c
+
+    lax.fori_loop(1, cols, step, 0)
+    make(col)
+    own = pltpu.make_async_copy(block.at[col], out_ref.at[col], own_sem)
+    own.start()
+    own.wait()
+
+    def finish(s, c):
+        send(s).wait()
+        return c
+
+    lax.fori_loop(1, cols, finish, 0)
+
+
+def back(modes, state, strain, rows, cols, nx, ny, nz):
+    groups, kb, _ = state.shape
+    yl = ny // cols
+    half = -(-(-(-ny // 3)) // yl)
+    cosine, sine = waves(np.arange(ny), np.arange(ny), ny)
+    kept = [j for j in range(cols) if j < half or j >= cols - half]
+    table = np.stack(
+        [
+            np.concatenate([m[:, j * yl : (j + 1) * yl] for m in (cosine, sine)], 1)
+            for j in kept
+        ]
+    )
+    whole = pl.BlockSpec(memory_space=pltpu.VMEM)
+    far = pl.BlockSpec(memory_space=pl.ANY)
+    return pl.pallas_call(
+        functools.partial(back_kernel, rows, cols, nx, ny, nz),
+        out_shape=jax.ShapeDtypeStruct((cols, groups, kb, yl), bf16),
+        in_specs=[whole, whole, whole, far],
+        out_specs=far,
+        scratch_shapes=[
+            pltpu.VMEM(table.shape, bf16),
+            pltpu.VMEM((n_pairs * 2 * nz * kb, ny), bf16),
+            pltpu.VMEM((cols, groups, kb, yl), bf16),
+            pltpu.SemaphoreType.DMA((len(kept),)),
+            pltpu.SemaphoreType.DMA((cols,)),
+            pltpu.SemaphoreType.DMA((cols,)),
+            pltpu.SemaphoreType.DMA,
+        ],
+        compiler_params=pltpu.CompilerParams(
+            collective_id=5, has_side_effects=True, vmem_limit_bytes=44 * 2**20
+        ),
+    )(modes, state, strain.reshape(1, 1), jnp.asarray(narrow(table)))
+
+
+def ahead_kernel(
+    rows, cols, ny, nz,
+    in_ref, offs_ref, table_ref, lines_ref, state_ref,
+    table, came, state, block,
+    table_sem, send_sem, recv_sem, own_sem, far_send, far_recv, far_own,
+):
+    row, col = lax.axis_index("row"), lax.axis_index("col")
+    count = rows * cols
+    me = row * cols + col
+    groups, kb, yl = in_ref.shape[1:]
+    gb = lines_ref.shape[2] // 3
+    gn = count // nz
+    tiles, _, wide = table_ref.shape
+    width = wide // 2
+    per = width // gb
+
+    def place(d):
+        return (d // cols, d % cols)
+
+    wait_all = greet_all(count, me, place)
+
+    def fetch(i):
+        return pltpu.make_async_copy(table_ref.at[i], table.at[i], table_sem.at[i])
+
+    def near(s):
+        other = (col + s) % cols
+        return pltpu.make_async_remote_copy(
+            src_ref=in_ref.at[other],
+            dst_ref=came.at[col],
+            send_sem=send_sem.at[s],
+            recv_sem=recv_sem.at[s],
+            device_id=(row, other),
+            device_id_type=pl.DeviceIdType.MESH,
+        )
+
+    wait_all()
+    for s in range(1, cols):
+        near(s).start()
+    own = pltpu.make_async_copy(in_ref.at[col], came.at[col], own_sem)
+    own.start()
+    for i in range(tiles):
+        fetch(i).start()
+    for i in range(tiles):
+        fetch(i).wait()
+    own.wait()
+    for s in range(1, cols):
+        near(s).wait()
+
+    def gather(g, c):
+        top = pl.multiple_of(g * kb, kb)
+        for s in range(cols):
+            state[pl.ds(top, kb), s * yl : (s + 1) * yl] = came[s, g]
+        return c
+
+    lax.fori_loop(0, groups, gather, 0)
+
+    def far(s):
+        other = (me + s) % count
+        return pltpu.make_async_remote_copy(
+            src_ref=block.at[other],
+            dst_ref=lines_ref.at[me],
+            send_sem=far_send.at[s],
+            recv_sem=far_recv.at[s],
+            device_id=place(other),
+            device_id_type=pl.DeviceIdType.MESH,
+        )
+
+    offs = offs_ref[...]
+
+    def tile(step, c):
+        t = (me // nz + step) % tiles
+        both = dot(state[...], table[t])
+        gy = t * width + lax.broadcasted_iota(jnp.int32, (kb, width), 1)
+        turn = (offs * gy) % ny
+        turn = jnp.where(turn < ny // 2, turn, turn - ny)
+        angle = (2.0 * math.pi / ny) * turn.astype(f32)
+        cosine, sine = jnp.cos(angle), jnp.sin(angle)
+        for c in range(3):
+            for z in range(nz):
+                a = both[((c * 2) * nz + z) * kb : ((c * 2) * nz + z + 1) * kb]
+                b = both[((c * 2 + 1) * nz + z) * kb : ((c * 2 + 1) * nz + z + 1) * kb]
+                real = a[:, :width] - b[:, width:]
+                imag = a[:, width:] + b[:, :width]
+                turned = (cosine * real + sine * imag, cosine * imag - sine * real)
+                for h in range(per):
+                    d = z * gn + t * per + h
+                    for p in range(2):
+                        block[d, p * kb : (p + 1) * kb, c * gb : (c + 1) * gb] = turned[p][
+                            :, h * gb : (h + 1) * gb
+                        ].astype(bf16)
+        for z in range(nz):
+            for h in range(per):
+                d = z * gn + t * per + h
+
+                @pl.when(d != me)
+                def _():
+                    far((d - me + count) % count).start()
+
+        return 0
+
+    lax.fori_loop(0, tiles, tile, 0)
+    far_copy = pltpu.make_async_copy(block.at[me], lines_ref.at[me], far_own)
+    far_copy.start()
+
+    def shift(g, c):
+        top = pl.multiple_of(g * kb, kb)
+        value = state[pl.ds(top, kb), :].astype(f32)
+        stride = 1
+        while stride < ny:
+            chosen = (offs // stride) % 2 == 1
+            value = jnp.where(chosen, pltpu.roll(value, ny - stride, 1), value)
+            stride *= 2
+        state_ref[g] = value.astype(bf16)
+        return c
+
+    lax.fori_loop(0, groups, shift, 0)
+    far_copy.wait()
+
+    def finish(s, c):
+        far(s).wait()
+        return c
+
+    lax.fori_loop(1, count, finish, 0)
+
+
+def ahead(parts, offs, rows, cols, ny, nz, gb):
+    groups, kb, yl = parts.shape[1:]
+    width = 2 * gb
+    cosine, sine = waves(np.arange(ny), np.arange(ny), ny)
+    table = np.stack(
+        [
+            np.concatenate([m[:, t : t + width] for m in (cosine, sine)], 1)
+            for t in range(0, ny, width)
+        ]
+    )
+    count = rows * cols
+    whole = pl.BlockSpec(memory_space=pltpu.VMEM)
+    far = pl.BlockSpec(memory_space=pl.ANY)
+    dma = pltpu.SemaphoreType.DMA
+    return pl.pallas_call(
+        functools.partial(ahead_kernel, rows, cols, ny, nz),
+        out_shape=(
+            jax.ShapeDtypeStruct((count, 2 * kb, 3 * gb), bf16),
+            jax.ShapeDtypeStruct((groups, kb, ny), bf16),
+        ),
+        in_specs=[far, whole, far],
+        out_specs=(far, whole),
+        scratch_shapes=[
+            pltpu.VMEM(table.shape, bf16),
+            pltpu.VMEM((cols, groups, kb, yl), bf16),
+            pltpu.VMEM((groups * kb, ny), bf16),
+            pltpu.VMEM((count, 2 * kb, 3 * gb), bf16),
+            dma((table.shape[0],)),
+            dma((cols,)),
+            dma((cols,)),
+            dma,
+            dma((count,)),
+            dma((count,)),
+            dma,
+        ],
+        compiler_params=pltpu.CompilerParams(
+            collective_id=6, has_side_effects=True, vmem_limit_bytes=44 * 2**20
+        ),
+    )(parts, offs.reshape(kb, 1), jnp.asarray(narrow(table)))
+
+
 def local(velocity_modes, offsets, shear_steps):
     nz, yl, kl = velocity_modes.shape[2:]
     rows, cols = lax.axis_size("row"), lax.axis_size("col")
@@ -175,18 +489,23 @@
     strain = shear_steps[0].astype(f32) / period - 0.5
 
     parts = velocity_modes.reshape(6 * nz, yl, cols, kb).transpose(2, 0, 3, 1)
-    parts = exchange(parts, rows, cols, False, 1)
     offs = lax.dynamic_slice(offsets, (col * kb,), (kb,))
-    remeshed = remesh(parts, offs)
-
-    every = np.arange(ny)
-    both = dot(remeshed.reshape(-1, ny), jnp.asarray(y_table(ny, every)))
-    both = both.reshape(3, 2, nz, kb, 2, ny)
-    real = both[:, 0, :, :, 0] - both[:, 1, :, :, 1]
-    imag = both[:, 0, :, :, 1] + both[:, 1, :, :, 0]
-    lines = jnp.stack([real, imag]).astype(bf16).reshape(2, 3, nz, kb, gn, gb)
-    lines = lines.transpose(2, 4, 0, 3, 1, 5).reshape(devices, 2 * kb, 3 * gb)
-    lines = exchange(lines, rows, cols, True, 2).reshape(2 * nk, 3 * gb)
+    aligned = kb % 16 == 0 and gb % 128 == 0 and yl % 128 == 0
+    if aligned:
+        lines, remeshed = ahead(parts, offs, rows, cols, ny, nz, gb)
+    else:
+        parts = exchange(parts, rows, cols, False, 1)
+        remeshed = remesh(parts, offs)
+
+        every = np.arange(ny)
+        both = dot(remeshed.reshape(-1, ny), jnp.asarray(y_table(ny, every)))
+        both = both.reshape(3, 2, nz, kb, 2, ny)
+        real = both[:, 0, :, :, 0] - both[:, 1, :, :, 1]
+        imag = both[:, 0, :, :, 1] + both[:, 1, :, :, 0]
+        lines = jnp.stack([real, imag]).astype(bf16).reshape(2, 3, nz, kb, gn, gb)
+        lines = lines.transpose(2, 4, 0, 3, 1, 5).reshape(devices, 2 * kb, 3 * gb)
+        lines = exchange(lines, rows, cols, True, 2)
+    lines = lines.reshape(2 * nk, 3 * gb)
 
     velocity = dot(jnp.asarray(x_inverse_table(nx, kb)), lines)
     v = [velocity[:, c * gb : (c + 1) * gb] for c in range(3)]
@@ -196,39 +515,42 @@
     x_modes = x_modes.reshape(kept, 2 * kb, n_pairs * gb)
     x_modes = exchange(x_modes, rows, cols, True, 3)
 
-    x_modes = x_modes.reshape(nz, gn, 2, kb, n_pairs, gb).transpose(4, 2, 0, 3, 1, 5)
-    low = -(-(-(-ny // 3)) // 128) * 128
-    near = np.concatenate([np.arange(low), np.arange(ny - low, ny)])
-    both = dot(x_modes.reshape(-1, ny), jnp.asarray(y_table(ny, near)))
-    both = both.reshape(n_pairs, 2, nz, kb, 2, 2 * low)
-    real = both[:, 0, :, :, 0] + both[:, 1, :, :, 1]
-    imag = both[:, 1, :, :, 0] - both[:, 0, :, :, 1]
-
-    kx = ((row * cols + col) * kb + jnp.arange(kb, dtype=jnp.int32))[:, None]
-    ys = jnp.concatenate(
-        [jnp.arange(low, dtype=jnp.int32), jnp.arange(-low, 0, dtype=jnp.int32)]
-    )[None, :]
-    k1 = 2.0 * math.pi * kx.astype(f32) / nx
-    k2 = 2.0 * math.pi * ys.astype(f32) / ny - strain * k1
-    retain = (3 * kx < nx) & (3 * jnp.abs(ys) < ny)
-    update = []
-    for l in range(3):
-        e0, e1 = pair_table[l]
-        flux_real = k1 * real[e0] + k2 * real[e1]
-        flux_imag = k1 * imag[e0] + k2 * imag[e1]
-        update.append(jnp.stack([flux_imag, -flux_real]))
-    update = jnp.where(retain, dt_step * jnp.stack(update), 0.0)
-    state = remeshed.reshape(3, 2, nz, kb, ny)
-    advanced = jnp.concatenate(
-        [
-            (state[..., :low].astype(f32) + update[..., :low]).astype(bf16),
-            state[..., low : ny - low],
-            (state[..., ny - low :].astype(f32) + update[..., low:]).astype(bf16),
-        ],
-        -1,
-    )
-    parts = advanced.reshape(6 * nz, kb, cols, yl).transpose(2, 0, 1, 3)
-    parts = exchange(parts, rows, cols, False, 4)
+    if aligned:
+        parts = back(x_modes, remeshed, strain, rows, cols, nx, ny, nz)
+    else:
+        x_modes = x_modes.reshape(nz, gn, 2, kb, n_pairs, gb).transpose(4, 2, 0, 3, 1, 5)
+        low = -(-(-(-ny // 3)) // 128) * 128
+        near = np.concatenate([np.arange(low), np.arange(ny - low, ny)])
+        both = dot(x_modes.reshape(-1, ny), jnp.asarray(y_table(ny, near)))
+        both = both.reshape(n_pairs, 2, nz, kb, 2, 2 * low)
+        real = both[:, 0, :, :, 0] + both[:, 1, :, :, 1]
+        imag = both[:, 1, :, :, 0] - both[:, 0, :, :, 1]
+
+        kx = ((row * cols + col) * kb + jnp.arange(kb, dtype=jnp.int32))[:, None]
+        ys = jnp.concatenate(
+            [jnp.arange(low, dtype=jnp.int32), jnp.arange(-low, 0, dtype=jnp.int32)]
+        )[None, :]
+        k1 = 2.0 * math.pi * kx.astype(f32) / nx
+        k2 = 2.0 * math.pi * ys.astype(f32) / ny - strain * k1
+        retain = (3 * kx < nx) & (3 * jnp.abs(ys) < ny)
+        update = []
+        for l in range(3):
+            e0, e1 = pair_table[l]
+            flux_real = k1 * real[e0] + k2 * real[e1]
+            flux_imag = k1 * imag[e0] + k2 * imag[e1]
+            update.append(jnp.stack([flux_imag, -flux_real]))
+        update = jnp.where(retain, dt_step * jnp.stack(update), 0.0)
+        state = remeshed.reshape(3, 2, nz, kb, ny)
+        advanced = jnp.concatenate(
+            [
+                (state[..., :low].astype(f32) + update[..., :low]).astype(bf16),
+                state[..., low : ny - low],
+                (state[..., ny - low :].astype(f32) + update[..., low:]).astype(bf16),
+            ],
+            -1,
+        )
+        parts = advanced.reshape(6 * nz, kb, cols, yl).transpose(2, 0, 1, 3)
+        parts = exchange(parts, rows, cols, False, 4)
     out = parts.transpose(1, 3, 0, 2)
     return out.reshape(3, 2, nz, yl, kl)
 

time: 242 us -> 176 us (0.73)
  matrix products: 36.3 us -> 7.97 us
  local copies, waits for them, and re-layouts: 31.4 us -> 8.45 us
  other arithmetic: 8.96 us -> 0.47 us
  Pallas kernels: 163 us -> 158 us
    pallas_call x4 -> x1, Pallas kernels: 152 us -> 65 us  [exchange(): pl.pallas_call(functools.partial(exchange_kernel, rows, cols, wide, kept,...]
    pallas_call x1 -> x2, Pallas kernels: 10.9 us -> 92.6 us  [the longest x1 58.4 us: ahead(): pl.pallas_call(functools.partial(ahead_kernel, rows, cols, ny, nz), out_s...]
    dot_general x4 -> x2, matrix products: 36.3 us -> 7.97 us  [dot(): return jnp.dot(a, b, preferred_element_type=f32)]
    reshape x5 -> x2, local copies, waits for them, and re-layouts: 11.8 us -> 0.16 us  [ahead(): offs.reshape(kb, 1)]
    add x4 -> x0, other arithmetic: 5.17 us -> none  [the longest x2 3.13 us: local(): real = both[:, 0, :, :, 0] + both[:, 1, :, :, 1]]
    transpose x1 -> x0, local copies, waits for them, and re-layouts: 4.15 us -> none  [local(): x_modes.reshape(nz, gn, 2, kb, n_pairs, gb).transpose(4, 2, 0, 3, 1, 5)]
    dot_general x1 -> x0, local copies, waits for them, and re-layouts: 3.09 us -> none  [dot(): return jnp.dot(a, b, preferred_element_type=f32)]
where the time goes in v2:
time: 176 us; the launch traced here: 175 us
  Pallas kernels  158 us (90%)
  local copies, waits for them, and re-layouts  8.45 us (5%)
  matrix products  7.97 us (5%)
    pallas_call x1, Pallas kernels, exchange(): pl.pallas_call(functools.partial(exchange_kernel, rows, cols, wide, kept,...  65 us
    pallas_call x1, Pallas kernels, ahead(): pl.pallas_call(functools.partial(ahead_kernel, rows, cols, ny, nz), out_s...  58.4 us
    pallas_call x1, Pallas kernels, back(): pl.pallas_call(functools.partial(back_kernel, rows, cols, nx, ny, nz), ou...  34.2 us
    dot_general x2, matrix products, dot(): return jnp.dot(a, b, preferred_element_type=f32)  7.97 us
    unnamed x15, local copies, waits for them, and re-layouts  4.16 us

profile of v2, /device:TPU:11, one launch (start us, length us, event | category | flops | bytes accessed | tf_op | source)
XLA Modules:
  0.0 175.4 jit_solution(3232509392490731122)
XLA Ops:
  0.0 0.0 copy-start
  0.0 0.7 copy-done
  0.7 0.1 dynamic-slice_bitcast_fusion
  0.8 0.1 copy.12.offs_ref
  0.8 1.7 copy.10
  2.6 0.0 slice-start
  2.6 0.2 copy.17
  2.7 0.0 slice-start.1
  2.8 0.0 slice-start.2
  2.8 58.4 %shard_map.73 = (bf16[32,64,384]{2,1,0:T(8,128)(2,1)S(1)}, bf16[12,32,2048]{2,1,0:T(8,128)(2,1)S(1)}) custom-call(bf16[8,12,32,256]{3,2,1,0:T(8,128)(2,1)S(1)} %bitcast.17, s32[32,1]{1,0:T(8,128)S(1)} %copy.12.offs_ref, bf16[8,2048,512]{2,1,0:T(8,128)(2,1)} %constant.26.clone.table_ref), custom_call_target="tpu_custom_call" | custom-call | tf_op jit(solution)/shard_map/pallas_call | solution.py:452
  61.2 0.0 slice-done
  61.2 0.0 slice-done.1
  61.2 0.0 slice-start.3
  61.2 3.6 %fusion.6 = f32[2048,384]{0,1:T(8,128)S(1)} fusion(bf16[2048,2048]{1,0:T(8,128)(2,1)S(1)} %bitcast.24, bf16[2048,384]{1,0:T(8,128)(2,1)S(1)} %bitcast.19), kind=kOutput, calls=%fused_computation.14 | convolution fusion | flops 3221225472 | bytes 13107200 | tf_op jit(solution)/shard_map/dot_general | solution.py:162
  64.9 0.1 fusion.1
  65.0 0.1 fusion.2
  65.1 0.1 fusion.3
  65.2 0.1 fusion.4
  65.3 0.1 fusion.5
  65.4 0.0 slice-done.2
  65.4 0.0 slice-done.3
  65.4 4.3 %fusion = bf16[1408,640]{0,1:T(8,128)(2,1)S(1)} fusion(bf16[2048,640]{0,1:T(8,128)(2,1)S(1)} %fusion.5, bf16[1408,2048]{1,0:T(8,128)(2,1)S(1)} %bitcast.26), kind=kOutput, calls=%fused_computation.1 | convolution fusion | flops 3691888640 | bytes 10190848 | tf_op jit(solution)/shard_map/dot_general | solution.py:162
  69.8 2.2 %copy.13 = bf16[1408,640]{1,0:T(8,128)(2,1)} copy(bf16[1408,640]{0,1:T(8,128)(2,1)S(1)} %fusion) | data formatting | bytes 3604480 | tf_op jit(solution)/shard_map/convert_element_type | solution.py:514
  72.0 65.0 %shard_map.74.modes_ref = bf16[32,64,640]{2,1,0:T(8,128)(2,1)} custom-call(bf16[22,64,640]{2,1,0:T(8,128)(2,1)} %bitcast.20), custom_call_target="tpu_custom_call" | custom-call | tf_op jit(solution)/shard_map/pallas_call | solution.py:119
  137.7 0.0 copy-start.2
  137.7 1.7 copy-done.2
  139.4 34.2 %shard_map.75 = bf16[8,12,32,256]{3,2,1,0:T(8,128)(2,1)S(1)} custom-call(bf16[32,64,640]{2,1,0:T(8,128)(2,1)S(1)} %copy-done.2, bf16[12,32,2048]{2,1,0:T(8,128)(2,1)S(1)} %get-tuple-element.8.state_ref, f32[1,1]{1,0:T(1,128)} %bitcast.6.strain_ref, bf16[6,2048,512]{2,1,0:T(8,128)(2,1)} %constant.29.clone.table_ref), custom_call_target="tpu_custom_call" | custom-call | tf_op jit(solution)/shard_map/pallas_call | solution.py:293
  173.6 0.0 copy-start.1
  173.6 0.2 copy.14
  173.8 1.6 copy.15
  175.4 0.0 copy-done.1
  (2 shorter events, 0.0 us)
Async XLA Ops:
  0.0 0.7 copy-start
  2.6 58.6 %slice-start = ((s8[8388608]{0:T(1024)(128)(4,1)}), s8[4194304]{0:T(1024)(128)(4,1)S(1)}, s32[]{:S(2)}) async-start(s8[8388608]{0:T(1024)(128)(4,1)} %bitcast.23), calls=%async_computation | async-start | bytes 8388608
  2.7 58.5 %slice-start.1 = ((s8[8388608]{0:T(1024)(128)(4,1)}), s8[4194304]{0:T(1024)(128)(4,1)S(1)}, s32[]{:S(2)}) async-start(s8[8388608]{0:T(1024)(128)(4,1)} %bitcast.23), calls=%async_computation.1 | async-start | bytes 8388608
  2.8 62.6 %slice-start.2 = ((s8[5767168]{0:T(1024)(128)(4,1)}), s8[4194304]{0:T(1024)(128)(4,1)S(1)}, s32[]{:S(2)}) async-start(s8[5767168]{0:T(1024)(128)(4,1)} %bitcast.25), calls=%async_computation.2 | async-start | bytes 8388608
  61.2 4.2 %slice-start.3 = ((s8[5767168]{0:T(1024)(128)(4,1)}), s8[1572864]{0:T(1024)(128)(4,1)S(1)}, s32[]{:S(2)}) async-start(s8[5767168]{0:T(1024)(128)(4,1)} %bitcast.25), calls=%async_computation.3 | async-start | bytes 3145728
  137.7 1.7 copy-start.2
  173.6 1.7 copy-start.1

commit v3 on v2

--- a/solution.py
+++ b/solution.py
@@ -179,53 +179,106 @@
 
 
 def back_kernel(
-    rows, cols, nx, ny, nz,
-    modes_ref, state_ref, strain_ref, table_ref, out_ref,
-    table, lines, block, table_sem, send_sem, recv_sem, own_sem,
+    rows, cols, nx, ny, nz, kept,
+    in_ref, state_ref, strain_ref, inverse_ref, forward_ref, table_ref, out_ref,
+    inverse, forward, table, products, away, modes, lines, block,
+    inverse_sem, forward_sem, table_sem,
+    far_send, far_recv, far_own, send_sem, recv_sem, own_sem,
 ):
     row, col = lax.axis_index("row"), lax.axis_index("col")
+    count = rows * cols
+    me = row * cols + col
     groups, kb, _ = state_ref.shape
     yl = ny // cols
     half = table_ref.shape[0] // 2
-    gn = modes_ref.shape[0] // nz
-    gb = modes_ref.shape[2] // n_pairs
-    first_k = (row * cols + col) * kb
-    wait_all = greet_all(cols, col, lambda d: (row, d))
-    live = 3 * first_k < nx
-
-    def fetch(i):
-        return pltpu.make_async_copy(table_ref.at[i], table.at[i], table_sem.at[i])
-
+    gn = count // nz
+    gb = in_ref.shape[1] // 3
+    first_k = me * kb
+    live = me < kept
+
+    def place(d):
+        return (d // cols, d % cols)
+
+    wait_all = greet_all(count, me, place)
+
+    def fetch(source, target, sem, i):
+        return pltpu.make_async_copy(source.at[i], target.at[i], sem.at[i])
+
+    triples = (
+        (inverse_ref, inverse, inverse_sem),
+        (forward_ref, forward, forward_sem),
+        (table_ref, table, table_sem),
+    )
+    for triple in triples:
+        for i in range(triple[0].shape[0]):
+            fetch(*triple, i).start()
+
+    piece = inverse_ref.shape[1]
+    for i in range(inverse_ref.shape[0]):
+        fetch(*triples[0], i).wait()
+        velocity = dot(inverse[i], in_ref[...])
+        v = [velocity[:, c * gb : (c + 1) * gb] for c in range(3)]
+        for e, (one, two) in enumerate(pairs):
+            products[i * piece : (i + 1) * piece, e * gb : (e + 1) * gb] = (
+                v[one] * v[two]
+            ).astype(bf16)
+    for i in range(forward_ref.shape[0]):
+        fetch(*triples[1], i).wait()
+    wait_all()
+
+    def far(s):
+        other = (me + s) % count
+        return pltpu.make_async_remote_copy(
+            src_ref=away.at[jnp.minimum(other, kept - 1)],
+            dst_ref=modes.at[me],
+            send_sem=far_send.at[s],
+            recv_sem=far_recv.at[s],
+            device_id=place(other),
+            device_id_type=pl.DeviceIdType.MESH,
+        )
+
+    tiles = forward_ref.shape[0]
+    per = forward_ref.shape[1] // (2 * kb)
+
+    def tile(step, c):
+        t = (me // per + 1 + step) % tiles
+        found = dot(forward[t], products[...]).astype(bf16)
+        for h in range(per):
+            away[t * per + h] = found[h * 2 * kb : (h + 1) * 2 * kb]
+        for h in range(per):
+            d = t * per + (me + h) % per
+
+            @pl.when((d != me) & (d < kept))
+            def _():
+                far((d - me + count) % count).start()
+
+        return c
+
+    lax.fori_loop(0, tiles, tile, 0)
+    far_copy = pltpu.make_async_copy(
+        away.at[jnp.minimum(me, kept - 1)], modes.at[me], far_own
+    )
+    far_copy.start()
     for i in range(2 * half):
-        fetch(i).start()
-    for e in range(n_pairs):
-        for p in range(2):
-            for z in range(nz):
-                top = ((e * 2 + p) * nz + z) * kb
-                for b in range(gn):
-                    lines[top : top + kb, b * gb : (b + 1) * gb] = modes_ref[
-                        z * gn + b, p * kb : (p + 1) * kb, e * gb : (e + 1) * gb
-                    ]
-    for i in range(2 * half):
-        fetch(i).wait()
-    wait_all()
-
-    def send(s):
+        fetch(*triples[2], i).wait()
+    far_copy.wait()
+
+    def send(z, s):
         other = (col + s) % cols
         return pltpu.make_async_remote_copy(
-            src_ref=block.at[other],
-            dst_ref=out_ref.at[col],
-            send_sem=send_sem.at[s],
-            recv_sem=recv_sem.at[s],
+            src_ref=block.at[z, other],
+            dst_ref=out_ref.at[col, z],
+            send_sem=send_sem.at[z, s],
+            recv_sem=recv_sem.at[z, s],
             device_id=(row, other),
             device_id_type=pl.DeviceIdType.MESH,
         )
 
-    def make(j):
-        kept = live & ((j < half) | (j >= cols - half))
+    def make(z, j):
+        used = live & ((j < half) | (j >= cols - half))
         columns = pl.ds(pl.multiple_of(j * yl, yl), yl)
 
-        @pl.when(kept)
+        @pl.when(used)
         def _():
             i = jnp.where(j < half, j, j - (cols - 2 * half))
             both = dot(lines[...], table[i])
@@ -235,79 +288,135 @@
             k1 = (2.0 * math.pi / nx) * kx.astype(f32)
             k2 = (2.0 * math.pi / ny) * ys.astype(f32) - strain_ref[...] * k1
             retain = (3 * kx < nx) & (3 * jnp.abs(ys) < ny)
-
-            def mode(e, z):
-                a = both[((e * 2) * nz + z) * kb : ((e * 2) * nz + z + 1) * kb]
-                b = both[((e * 2 + 1) * nz + z) * kb : ((e * 2 + 1) * nz + z + 1) * kb]
-                return a[:, :yl] + b[:, yl:], b[:, :yl] - a[:, yl:]
-
-            for z in range(nz):
-                found = [mode(e, z) for e in range(n_pairs)]
-                for l in range(3):
-                    e0, e1 = pair_table[l]
-                    flux_real = k1 * found[e0][0] + k2 * found[e1][0]
-                    flux_imag = k1 * found[e0][1] + k2 * found[e1][1]
-                    for p, update in ((0, flux_imag), (1, -flux_real)):
-                        g = (l * 2 + p) * nz + z
-                        state = state_ref[g, :, columns].astype(f32)
-                        change = jnp.where(retain, dt_step * update, 0.0)
-                        block[j, g] = (state + change).astype(bf16)
-
-        @pl.when(jnp.logical_not(kept))
+            found = []
+            for e in range(n_pairs):
+                a = both[2 * e * kb : (2 * e + 1) * kb]
+                b = both[(2 * e + 1) * kb : (2 * e + 2) * kb]
+                found.append((a[:, :yl] + b[:, yl:], b[:, :yl] - a[:, yl:]))
+            for l in range(3):
+                e0, e1 = pair_table[l]
+                flux_real = k1 * found[e0][0] + k2 * found[e1][0]
+                flux_imag = k1 * found[e0][1] + k2 * found[e1][1]
+                for p, update in ((0, flux_imag), (1, -flux_real)):
+                    state = state_ref[(l * 2 + p) * nz + z, :, columns].astype(f32)
+                    change = jnp.where(retain, dt_step * update, 0.0)
+                    block[z, j, l * 2 + p] = (state + change).astype(bf16)
+
+        @pl.when(jnp.logical_not(used))
         def _():
-            for g in range(groups):
-                block[j, g] = state_ref[g, :, columns]
-
-    def step(s, c):
-        make((col + s) % cols)
-        send(s).start()
-        return c
-
-    lax.fori_loop(1, cols, step, 0)
-    make(col)
-    own = pltpu.make_async_copy(block.at[col], out_ref.at[col], own_sem)
-    own.start()
-    own.wait()
+            for g in range(groups // nz):
+                block[z, j, g] = state_ref[g * nz + z, :, columns]
+
+    def plane(turn, c):
+        z = (row * nz // rows + turn) % nz
+
+        @pl.when(live)
+        def _():
+            def arrive(b, c):
+                s = (me + count - (z * gn + b)) % count
+
+                @pl.when(s != 0)
+                def _():
+                    far(s).wait_recv()
+
+                return c
+
+            lax.fori_loop(0, gn, arrive, 0)
+            for b in range(gn):
+                for e in range(n_pairs):
+                    lines[2 * e * kb : 2 * (e + 1) * kb, b * gb : (b + 1) * gb] = modes[
+                        z * gn + b, :, e * gb : (e + 1) * gb
+                    ]
+
+        def step(s, c):
+            make(z, (col + s) % cols)
+            send(z, s).start()
+            return c
+
+        lax.fori_loop(1, cols, step, 0)
+        make(z, col)
+        own = pltpu.make_async_copy(block.at[z, col], out_ref.at[col, z], own_sem)
+        own.start()
+        own.wait()
+        return c
+
+    lax.fori_loop(0, nz, plane, 0)
 
     def finish(s, c):
-        send(s).wait()
+        for z in range(nz):
+            send(z, s).wait()
         return c
 
     lax.fori_loop(1, cols, finish, 0)
 
-
-def back(modes, state, strain, rows, cols, nx, ny, nz):
+    def sent(s, c):
+        @pl.when((me + s) % count < kept)
+        def _():
+            far(s).wait_send()
+
+        return c
+
+    lax.fori_loop(1, count, sent, 0)
+
+
+def back(arrived, state, strain, rows, cols, nx, ny, nz):
     groups, kb, _ = state.shape
     yl = ny // cols
+    count = rows * cols
+    gb = arrived.shape[1] // 3
     half = -(-(-(-ny // 3)) // yl)
     cosine, sine = waves(np.arange(ny), np.arange(ny), ny)
-    kept = [j for j in range(cols) if j < half or j >= cols - half]
     table = np.stack(
         [
             np.concatenate([m[:, j * yl : (j + 1) * yl] for m in (cosine, sine)], 1)
-            for j in kept
+            for j in range(cols)
+            if j < half or j >= cols - half
         ]
     )
+    inverse = x_inverse_table(nx, kb).reshape(4, nx // 4, nx)
+    kept = -(-(-(-nx // 3)) // kb)
+    per = 4
+    tiles = -(-kept // per)
+    forward = x_forward_table(nx, kb, tiles * per).reshape(tiles, per * 2 * kb, nx)
     whole = pl.BlockSpec(memory_space=pltpu.VMEM)
     far = pl.BlockSpec(memory_space=pl.ANY)
+    dma = pltpu.SemaphoreType.DMA
+    vmem = lambda *shape: pltpu.VMEM(shape, bf16)
     return pl.pallas_call(
-        functools.partial(back_kernel, rows, cols, nx, ny, nz),
-        out_shape=jax.ShapeDtypeStruct((cols, groups, kb, yl), bf16),
-        in_specs=[whole, whole, whole, far],
+        functools.partial(back_kernel, rows, cols, nx, ny, nz, kept),
+        out_shape=jax.ShapeDtypeStruct((cols, nz, groups // nz, kb, yl), bf16),
+        in_specs=[whole, whole, whole, far, far, far],
         out_specs=far,
         scratch_shapes=[
-            pltpu.VMEM(table.shape, bf16),
-            pltpu.VMEM((n_pairs * 2 * nz * kb, ny), bf16),
-            pltpu.VMEM((cols, groups, kb, yl), bf16),
-            pltpu.SemaphoreType.DMA((len(kept),)),
-            pltpu.SemaphoreType.DMA((cols,)),
-            pltpu.SemaphoreType.DMA((cols,)),
-            pltpu.SemaphoreType.DMA,
+            vmem(*inverse.shape),
+            vmem(*forward.shape),
+            vmem(*table.shape),
+            vmem(nx, n_pairs * gb),
+            vmem(tiles * per, 2 * kb, n_pairs * gb),
+            vmem(count, 2 * kb, n_pairs * gb),
+            vmem(n_pairs * 2 * kb, ny),
+            vmem(nz, cols, groups // nz, kb, yl),
+            dma((inverse.shape[0],)),
+            dma((tiles,)),
+            dma((table.shape[0],)),
+            dma((count,)),
+            dma((count,)),
+            dma,
+            dma((nz, cols)),
+            dma((nz, cols)),
+            dma,
         ],
         compiler_params=pltpu.CompilerParams(
-            collective_id=5, has_side_effects=True, vmem_limit_bytes=44 * 2**20
+            collective_id=7, has_side_effects=True, vmem_limit_bytes=54 * 2**20
         ),
-    )(modes, state, strain.reshape(1, 1), jnp.asarray(narrow(table)))
+    )(
+        arrived,
+        state,
+        strain.reshape(1, 1),
+        jnp.asarray(inverse),
+        jnp.asarray(forward),
+        jnp.asarray(narrow(table)),
+    )
 
 
 def ahead_kernel(
@@ -507,17 +616,19 @@
         lines = exchange(lines, rows, cols, True, 2)
     lines = lines.reshape(2 * nk, 3 * gb)
 
-    velocity = dot(jnp.asarray(x_inverse_table(nx, kb)), lines)
-    v = [velocity[:, c * gb : (c + 1) * gb] for c in range(3)]
-    products = jnp.concatenate([(v[a] * v[b]).astype(bf16) for a, b in pairs], 1)
-    kept = -(-(-(-nx // 3)) // kb)
-    x_modes = dot(jnp.asarray(x_forward_table(nx, kb, kept)), products).astype(bf16)
-    x_modes = x_modes.reshape(kept, 2 * kb, n_pairs * gb)
-    x_modes = exchange(x_modes, rows, cols, True, 3)
-
     if aligned:
-        parts = back(x_modes, remeshed, strain, rows, cols, nx, ny, nz)
+        parts = back(lines, remeshed, strain, rows, cols, nx, ny, nz)
+        parts = parts.transpose(2, 1, 4, 0, 3)
+        return parts.reshape(3, 2, nz, yl, kl)
     else:
+        velocity = dot(jnp.asarray(x_inverse_table(nx, kb)), lines)
+        v = [velocity[:, c * gb : (c + 1) * gb] for c in range(3)]
+        products = jnp.concatenate([(v[a] * v[b]).astype(bf16) for a, b in pairs], 1)
+        kept = -(-(-(-nx // 3)) // kb)
+        x_modes = dot(jnp.asarray(x_forward_table(nx, kb, kept)), products).astype(bf16)
+        x_modes = x_modes.reshape(kept, 2 * kb, n_pairs * gb)
+        x_modes = exchange(x_modes, rows, cols, True, 3)
+
         x_modes = x_modes.reshape(nz, gn, 2, kb, n_pairs, gb).transpose(4, 2, 0, 3, 1, 5)
         low = -(-(-(-ny // 3)) // 128) * 128
         near = np.concatenate([np.arange(low), np.arange(ny - low, ny)])

time: 176 us -> 156 us (0.89)
  Pallas kernels: 158 us -> 147 us
  matrix products: 7.97 us -> 0 us
    pallas_call x2 -> x1, Pallas kernels: 99.2 us -> 89 us  [back(): pl.pallas_call(functools.partial(back_kernel, rows, cols, nx, ny, nz, kep...]
    dot_general x2 -> x0, matrix products: 7.97 us -> none  [dot(): return jnp.dot(a, b, preferred_element_type=f32)]
    convert_element_type x1 -> x0, local copies, waits for them, and re-layouts: 2.24 us -> none  [local(): dot(jnp.asarray(x_forward_table(nx, kb, kept)), products).astype(bf16)]
    unnamed x15 -> x7, local copies, waits for them, and re-layouts: 4.16 us -> 4.69 us
where the time goes in v3:
time: 156 us
  Pallas kernels  147 us (94%)
  local copies, waits for them, and re-layouts  8.12 us (5%)
    pallas_call x1, Pallas kernels, back(): pl.pallas_call(functools.partial(back_kernel, rows, cols, nx, ny, nz, kep...  89 us
    pallas_call x1, Pallas kernels, ahead(): pl.pallas_call(functools.partial(ahead_kernel, rows, cols, ny, nz), out_s...  58.4 us
    unnamed x7, local copies, waits for them, and re-layouts  4.69 us

profile of v3, /device:TPU:11, one launch (start us, length us, event | category | flops | bytes accessed | tf_op | source)
XLA Modules:
  0.0 156.3 jit_solution(11848267597287288102)
XLA Ops:
  0.0 0.0 copy-start
  0.0 0.7 copy-done
  0.7 0.1 dynamic-slice_bitcast_fusion
  0.8 0.1 copy.11.offs_ref
  0.8 1.7 %copy.9 = bf16[3,2,2,256,256]{3,4,2,1,0:T(8,128)(2,1)S(1)} copy(bf16[3,2,2,256,256]{4,3,2,1,0:T(8,128)(2,1)} %param.7) | data formatting | bytes 3145728 | tf_op args[0]
  2.6 0.1 copy.15
  2.7 58.4 %shard_map.73 = (bf16[32,64,384]{2,1,0:T(8,128)(2,1)S(1)}, bf16[12,32,2048]{2,1,0:T(8,128)(2,1)S(1)}) custom-call(bf16[8,12,32,256]{3,2,1,0:T(8,128)(2,1)S(1)} %bitcast.10, s32[32,1]{1,0:T(8,128)S(1)} %copy.11.offs_ref, bf16[8,2048,512]{2,1,0:T(8,128)(2,1)} %constant.26.clone.table_ref), custom_call_target="tpu_custom_call" | custom-call | tf_op jit(solution)/shard_map/pallas_call | solution.py:561
  61.1 0.0 copy-start.1
  61.1 1.1 copy-done.1
  62.3 0.0 copy-start.2
  62.3 1.2 copy-done.2
  64.1 89.0 %shard_map.74 = bf16[8,2,6,32,256]{4,3,2,1,0:T(8,128)(2,1)} custom-call(bf16[2048,384]{1,0:T(8,128)(2,1)} %bitcast.11, bf16[12,32,2048]{2,1,0:T(8,128)(2,1)} %copy-done.2, f32[1,1]{1,0:T(1,128)} %bitcast.4.strain_ref, bf16[4,512,2048]{2,1,0:T(8,128)(2,1)} %constant.27.clone.inverse_ref, bf16[6,256,2048]{2,1,0:T(8,128)(2,1)} %constant.28.clone.forward_ref, ...), custom_call_target="tpu_custom_call" | custom-call | tf_op jit(solution)/shard_map/pallas_call | solution.py:385
  153.1 1.6 copy.12
  154.7 1.6 %copy.13 = bf16[3,2,2,256,256]{4,3,2,1,0:T(8,128)(2,1)} copy(bf16[3,2,2,256,256]{3,4,2,1,0:T(8,128)(2,1)S(1)} %bitcast.13) | data formatting | bytes 3145728 | tf_op jit(solution)/shard_map/reshape | solution.py:622
Async XLA Ops:
  0.0 0.7 copy-start
  61.1 1.1 copy-start.1
  62.3 1.2 copy-start.2
